TPU v7x, 32 devices: a whole 2x2x4 slice. The times are simulated.
32 devices in a mesh: slab: 4 (over x, core), wide: 8 (over z, y).
Axes of the slice: x: 2, y: 2, z: 4, core: 2. Of those that a mesh axis runs over, the one named last changes fastest.
Arguments:
- orbitals: float32 [256, 128, 128, 128], P(None, 'slab', 'wide'), may hold values from -6 to 6
- points: int32 [512], replicated, may hold values from 0 to 2097151, as said below
Outputs:
- potential: float32 [32, 128, 128, 128], P(None, 'slab', 'wide')
Inputs may be any that keep to these rules, and one draw needn't show every extreme that they name: `points`: the 512 indices are distinct; how many fall in the cells of one device differs strongly between devices.
All inputs are finite; a program needn't handle non-finite values.
Results may differ from a plain program's by a relative error of at most 0.00014.
Values sent between devices are 32-bit elements; how exact they have to be, the bound alone decides.
A program may use at most 256 MiB of HBM per device.

v0:
```python
import math

import jax
import jax.numpy as jnp
from jax import lax
from jax.sharding import PartitionSpec as P

VEC_DEV = 1


highest = lax.Precision.HIGHEST


def tables(length):
    index = jnp.arange(length, dtype=jnp.int32)
    phase = index[:, None] * index[None, :] % length
    angle = phase.astype(jnp.float32) * (2.0 * math.pi / length)
    return (jnp.cos(angle), jnp.sin(angle))


def contract(values, table, axis_pos):
    letters = "abcd"[: values.ndim]
    target = letters[:axis_pos] + "k" + letters[axis_pos + 1 :]
    return jnp.einsum(
        letters + "," + letters[axis_pos] + "k->" + target, values, table, precision=highest
    )


def rotate(stacked, axis_pos, sign, cosine, sine):
    real_part = stacked[0]
    imag_part = stacked[1]
    new_real = contract(real_part, cosine, axis_pos) - sign * contract(imag_part, sine, axis_pos)
    new_imag = contract(imag_part, cosine, axis_pos) + sign * contract(real_part, sine, axis_pos)
    return jnp.stack([new_real, new_imag])


def coulomb(zfreq, yfreq, xfreq, length, factor):

    def squared(index):
        signed = jnp.where(index > length // 2, index - length, index).astype(jnp.float32) * (
            2.0 * math.pi / length
        )
        return signed * signed

    total = (
        squared(zfreq)[:, None, None]
        + squared(yfreq)[None, :, None]
        + squared(xfreq)[None, None, :]
    )
    safe = jnp.where(total > 0, total, 1.0)
    return jnp.where(total > 0, 4.0 * math.pi * factor / safe, 0.0)


def per_device(orbitals, points):
    norbit, depth, rows, grid = orbitals.shape
    npoint = points.shape[0]
    slab_count = lax.axis_size("slab")
    wide_count = lax.axis_size("wide")
    slab_index = lax.axis_index("slab")
    wide_index = lax.axis_index("wide")
    cells = depth * rows * grid
    flat = orbitals.reshape(norbit, cells)
    zcoord = points // (grid * grid)
    ycoord = points // grid % grid
    xcoord = points % grid
    owned = (zcoord // depth == slab_index) & (ycoord // rows == wide_index)
    offset = ((zcoord - slab_index * depth) * rows + (ycoord - wide_index * rows)) * grid + xcoord
    offset = jnp.where(owned, offset, 0)
    picked = jnp.take(flat, offset, axis=1) * owned.astype(jnp.float32)[None, :]
    sampled = lax.psum(picked, ("slab", "wide"))
    correlation = jnp.dot(sampled.T, sampled, precision=highest)
    gram = correlation * correlation
    gram = gram + 0.01 * jnp.mean(jnp.diagonal(gram)) * jnp.eye(npoint, dtype=jnp.float32)
    factor = jnp.linalg.cholesky(gram)
    devices = slab_count * wide_count
    vectors = VEC_DEV * devices
    coeffs = jax.scipy.linalg.cho_solve((factor, True), jnp.eye(npoint, vectors, dtype=jnp.float32))
    coeff_rows = coeffs.T
    sampled_rows = sampled.T
    width = math.gcd(cells, 4096)

    def fit_block(turn, fitted):
        start = turn * width
        block = lax.dynamic_slice_in_dim(flat, start, width, 1)
        pairs = jnp.dot(sampled_rows, block, precision=highest)
        piece = jnp.dot(coeff_rows, pairs * pairs, precision=highest)
        return lax.dynamic_update_slice_in_dim(fitted, piece, start, 1)

    fitting = lax.fori_loop(0, cells // width, fit_block, jnp.zeros((vectors, cells), jnp.float32))
    cosine, sine = tables(grid)
    scale = 1.0 / float(grid * grid * grid)
    freqs = jnp.arange(grid, dtype=jnp.int32)
    own = vectors // devices
    shaped = fitting.reshape(vectors, 1, depth, rows, grid)
    shaped = lax.all_to_all(shaped, ("slab", "wide"), split_axis=0, concat_axis=1, tiled=True)
    whole = shaped.reshape(own, slab_count, wide_count, depth, rows, grid)
    whole = whole.transpose(0, 1, 3, 2, 4, 5).reshape(own, grid, grid, grid)
    spectrum = jnp.stack([contract(whole, cosine, 3), -contract(whole, sine, 3)])
    spectrum = rotate(spectrum, 2, -1.0, cosine, sine)
    spectrum = rotate(spectrum, 1, -1.0, cosine, sine)
    spectrum = spectrum * coulomb(freqs, freqs, freqs, grid, scale)
    spectrum = rotate(spectrum, 1, 1.0, cosine, sine)
    spectrum = rotate(spectrum, 2, 1.0, cosine, sine)
    real_field = contract(spectrum[0], cosine, 3) - contract(spectrum[1], sine, 3)
    back = real_field.reshape(own, slab_count, depth, wide_count, rows, grid)
    back = back.transpose(0, 1, 3, 2, 4, 5).reshape(own, devices, depth, rows, grid)
    back = lax.all_to_all(back, ("slab", "wide"), split_axis=1, concat_axis=0, tiled=True)
    return back.reshape(vectors, depth, rows, grid)


def solution(mesh):
    placed = (P(None, "slab", "wide", None), P())
    return jax.shard_map(
        per_device,
        mesh=mesh,
        in_specs=placed,
        out_specs=P(None, "slab", "wide", None),
        check_vma=False,
    )
```

profile of v0, /device:TPU:0, one launch (start us, length us, event | category | flops | bytes accessed | tf_op | source)
XLA Modules:
  0.0 1313.8 jit_solution(13069238131313387668)
XLA Ops:
  7.3 66.8 %copy.60 = f32[256,32,16,128]{0,3,2,1:T(8,128)} copy(f32[256,32,16,128]{3,2,1,0:T(8,128)} %param.4) | data formatting | bytes 134217728 | tf_op args[0]
  74.1 17.3 %gather_fusion = f32[512,256]{1,0:T(8,128)S(1)} fusion(f32[256,65536]{0,1:T(8,128)} %bitcast.5, s32[1024]{0:T(1024)S(1)} %pad_clamp_fusion), kind=kCustom, calls=%fused_computation | custom fusion | bytes 1050624 | tf_op jit(solution)/shard_map/jit(_take)/gather | solution.py:69
  92.4 133.5 %all-reduce.3.cloned.1.call-done = f32[256,512]{0,1:T(8,128)} async-done(((f32[256,512]{0,1:T(8,128)}), f32[256,512]{0,1:T(8,128)}) %all-reduce.3.cloned.1.call-update) | async-done | bytes 524304 | tf_op jit(solution)/shard_map/psum | solution.py:70
  234.7 11.7 cholesky.103
  246.6 9.8 custom-call.34
  257.1 11.7 cholesky.215
  268.8 10.2 custom-call.35
  279.7 11.7 cholesky.236
  292.1 9.8 custom-call.36
  302.5 11.7 cholesky.253
  318.3 8.1 while.15
  326.4 39.5 %custom-call.37 = f32[4,128,128]{1,2,0:T(8,128)S(1)} custom-call(f32[4,128,128]{2,1,0:T(8,128)S(1)} %get-tuple-element.107), custom_call_target="InvertDiagBlocksLowerTriangular" | custom-call | tf_op jit(solution)/shard_map/jit(_cho_solve)/triangular_solve | solution.py:77
  372.9 276.2 %while.14 = (s32[]{:T(128)}, f32[32,65536]{1,0:T(8,128)}, f32[256,65536]{0,1:T(8,128)}, f32[512,256]{1,0:T(8,128)S(1)}, f32[32,512]{1,0:T(8,128)S(1)}, /*index=5*/s32[]{:T(128)}, s32[]{:T(128)}, s32[]{:T(128)}, s32[]{:T(128)}) while((s32[]{:T(128)}, f32[32,65536]{1,0:T(8,128)}, f32[256,65536]{0,1:T(8,128)}, f32[512,256]{1,0:T(8,128)S(1)}, ...), condition=%wide.region_11.12_spmd, body=%wide.region_10.11_spmd.sunk | while | flops 7249854464 | bytes 22085780 | solution.py:89
  372.9 8.7 fusion.280
  381.6 8.6 fusion.281
  390.2 8.7 fusion.280
  398.9 8.6 fusion.281
  407.4 8.7 fusion.280
  416.1 8.6 fusion.281
  424.7 8.7 fusion.280
  433.4 8.6 fusion.281
  441.9 8.7 fusion.280
  450.6 8.6 fusion.281
  459.2 8.7 fusion.280
  467.9 8.6 fusion.281
  476.5 8.7 fusion.280
  485.2 8.6 fusion.281
  493.7 8.7 fusion.280
  502.4 8.6 fusion.281
  511.0 8.7 fusion.280
  519.7 8.6 fusion.281
  528.3 8.7 fusion.280
  537.0 8.6 fusion.281
  545.5 8.7 fusion.280
  554.2 8.6 fusion.281
  562.8 8.7 fusion.280
  571.5 8.6 fusion.281
  580.1 8.7 fusion.280
  588.8 8.6 fusion.281
  597.3 8.7 fusion.280
  606.0 8.6 fusion.281
  614.6 8.7 fusion.280
  623.3 8.6 fusion.281
  631.8 8.7 fusion.280
  640.5 8.6 fusion.281
  649.1 8.1 copy.122
  667.9 182.6 %all-to-all-done = f32[32,1,32,16,128]{4,3,2,1,0:T(8,128)} async-done(((f32[32,1,32,16,128]{4,3,2,1,0:T(8,128)}), f32[32,1,32,16,128]{4,3,2,1,0:T(8,128)}, u32[]{:S(2)}, u32[]{:S(2)}) %all-to-all-start) | async-done | bytes 8388640 | tf_op jit(solution)/shard_map/all_to_all | solution.py:95
  878.2 10.2 fusion.78
  888.4 10.4 add_bitcast_fusion.1
  898.8 17.5 %fusion.33 = f32[128,128,128]{2,0,1:T(8,128)} fusion(f32[128,128,128]{2,1,0:T(8,128)S(1)} %add_bitcast_fusion.1), kind=kOutput, calls=%fused_computation.42 | convolution fusion | flops 3221454848 | bytes 16777216 | tf_op jit(solution)/shard_map/abcd,bk->akcd/dot_general | solution.py:24
  916.3 18.0 %fusion.31 = f32[128,128,128]{2,0,1:T(8,128)} fusion(f32[128,128,128]{2,1,0:T(8,128)S(1)} %add_bitcast_fusion.1), kind=kOutput, calls=%fused_computation.40 | convolution fusion | flops 3221454848 | bytes 16777216 | tf_op jit(solution)/shard_map/abcd,bk->akcd/dot_general | solution.py:24
  934.4 8.4 subtract_bitcast_fusion.1
  942.8 18.2 %subtract_bitcast_fusion = f32[1,1,128,128,128]{4,2,3,1,0:T(8,128)S(1)} fusion(f32[128,128,128]{2,0,1:T(8,128)} %fusion.33, f32[128,128,128]{2,1,0:T(8,128)S(1)} %subtract_bitcast_fusion.1), kind=kOutput, calls=%fused_computation.25 | convolution fusion | flops 3225649152 | bytes 25165824 | tf_op jit(solution)/shard_map/abcd,bk->akcd/dot_general | solution.py:24
  960.9 17.9 %add_bitcast_fusion = f32[1,1,128,128,128]{4,2,3,1,0:T(8,128)} fusion(f32[128,128,128]{2,0,1:T(8,128)S(1)} %copy-done, f32[128,128,128]{2,1,0:T(8,128)S(1)} %subtract_bitcast_fusion.1), kind=kOutput, calls=%fused_computation.24 | convolution fusion | flops 3225649152 | bytes 25165824 | tf_op jit(solution)/shard_map/abcd,bk->akcd/dot_general | solution.py:24
  986.5 10.4 fusion.20
  996.9 10.0 fusion.19
  1006.9 10.4 fusion.51
  1017.3 17.3 %fusion.27 = f32[128,128,128]{2,0,1:T(8,128)} fusion(f32[128,128,128]{2,0,1:T(8,128)S(1)} %fusion.51), kind=kOutput, calls=%fused_computation.36 | convolution fusion | flops 3221454848 | bytes 16777216 | tf_op jit(solution)/shard_map/abcd,ck->abkd/dot_general | solution.py:24
  1034.6 17.5 %fusion.29 = f32[128,128,128]{2,0,1:T(8,128)} fusion(f32[128,128,128]{2,0,1:T(8,128)S(1)} %fusion.51), kind=kOutput, calls=%fused_computation.38 | convolution fusion | flops 3221454848 | bytes 16777216 | tf_op jit(solution)/shard_map/abcd,ck->abkd/dot_general | solution.py:24
  1052.1 10.6 fusion.52
  1062.7 12.7 fusion.23
  1075.4 17.5 %fusion.25 = f32[128,128,128]{2,0,1:T(8,128)} fusion(f32[128,128,128]{2,0,1:T(8,128)S(1)} %fusion.52), kind=kOutput, calls=%fused_computation.34 | convolution fusion | flops 3221454848 | bytes 16777216 | tf_op jit(solution)/shard_map/abcd,ck->abkd/dot_general | solution.py:24
  1100.4 11.9 fusion.53
  1116.6 186.7 %all_to_all.8 = f32[1,32,32,16,128]{4,3,2,0,1:T(8,128)S(1)} all-to-all(f32[1,32,32,16,128]{4,3,2,0,1:T(8,128)S(1)} %bitcast.199), channel_id=1, replica_groups=mesh['slab'=4,'wide'=8] {'slab','wide'}, dimensions={1} | all-to-all | bytes 16777216 | tf_op jit(solution)/shard_map/all_to_all | solution.py:107
  (86 shorter events, 90.0 us)
Async XLA Ops:
  6.5 219.4 %all-reduce.3.cloned.1.call-start = ((), (), s32[]{:S(2)}) async-start(), calls=%async_computation.2 | async-start | bytes 1048576 | tf_op jit(solution)/shard_map/psum | solution.py:70
  256.4 116.5 %copy-start.2 = (f32[256,512]{0,1:T(8,128)S(1)}, f32[256,512]{0,1:T(8,128)}, u32[]{:S(2)}) copy-start(f32[256,512]{0,1:T(8,128)} %all-reduce.3.cloned.1.call-done) | copy-start | bytes 1572868
  657.2 193.2 %all-to-all-start = ((f32[32,1,32,16,128]{4,3,2,1,0:T(8,128)}), f32[32,1,32,16,128]{4,3,2,1,0:T(8,128)}, u32[]{:S(2)}, u32[]{:S(2)}) async-start(f32[32,1,32,16,128]{4,3,2,1,0:T(8,128)} %bitcast.198), calls=%async_computation | async-start | bytes 16777216 | tf_op jit(solution)/shard_map/all_to_all | solution.py:95
  942.7 18.2 %copy-start = (f32[128,128,128]{2,0,1:T(8,128)S(1)}, f32[128,128,128]{2,0,1:T(8,128)}, u32[]{:S(2)}) copy-start(f32[128,128,128]{2,0,1:T(8,128)} %fusion.31) | copy-start | bytes 25165828
  1062.7 30.3 %slice-start = ((s8[8388608]{0:T(1024)(128)(4,1)}), s8[4194304]{0:T(1024)(128)(4,1)S(1)}, s32[]{:S(2)}) async-start(s8[8388608]{0:T(1024)(128)(4,1)} %bitcast.196), calls=%async_computation.3 | async-start | bytes 8388608
  1075.4 17.6 %slice-start.1 = ((s8[8388608]{0:T(1024)(128)(4,1)}), s8[4194304]{0:T(1024)(128)(4,1)S(1)}, s32[]{:S(2)}) async-start(s8[8388608]{0:T(1024)(128)(4,1)} %bitcast.196), calls=%async_computation.4 | async-start | bytes 8388608
  1093.0 7.3 copy-start.1
Sparse Core Ops, SparseCore 0:
  92.5 133.3 all-reduce.2
where the time goes:
time: 1320 us; the launch traced here: 1310 us
  matrix products  533 us (40%)
  waiting for transfers between devices  316 us (24%)
  blocking collectives  187 us (14%)
  other arithmetic  135 us (10%)
  local copies, waits for them, and re-layouts  122 us (9%)
  between operations  17.4 us (1%)
    dot_general x20, matrix products, contract(): jnp.einsum(letters + ',' + letters[axis_pos] + 'k->' + target, values, ta...  249 us
    all_to_all x1, blocking collectives, per_device(): lax.all_to_all(back, ('slab', 'wide'), split_axis=1, concat_axis=0, tiled...  187 us
    all_to_all x1, waiting for transfers between devices, per_device(): lax.all_to_all(shaped, ('slab', 'wide'), split_axis=0, concat_axis=1, til...  183 us
    dot_general x16, matrix products, fit_block(): pairs = jnp.dot(sampled_rows, block, precision=highest)  139 us
    dot_general x16, matrix products, fit_block(): piece = jnp.dot(coeff_rows, pairs * pairs, precision=highest)  137 us
    psum x1, waiting for transfers between devices, per_device(): sampled = lax.psum(picked, ('slab', 'wide'))  133 us
    another operation x14, other arithmetic, per_device(): factor = jnp.linalg.cholesky(gram)  78.8 us
    unnamed x13, local copies, waits for them, and re-layouts  78.3 us
  transfers between devices with their start and end apart: 2, of which 2 were waited for; matrix products, arithmetic and copies ran while one was open for 1% of the time, Pallas kernels for 0%

commit v1 on v0

v1 whole, which is shorter than its diff:
```python
import functools
import math

import jax
import jax.numpy as jnp
import ml_dtypes
import numpy as np
from jax import lax
from jax.experimental import pallas as pl
from jax.experimental.pallas import tpu as pltpu
from jax.sharding import PartitionSpec as P

highest = lax.Precision.HIGHEST
MESH = pl.DeviceIdType.MESH
MIB = 1 << 20
f32 = jnp.float32
bf16 = jnp.bfloat16


def split(values):
    high = values.astype(bf16)
    low = (values - high.astype(f32)).astype(bf16)
    return high, low


def mul(left, right):
    return jnp.dot(left, right, preferred_element_type=f32)


def pick_kernel(slots, code_ref, orb_ref, out_ref, owned_ref, buf, sem):
    npoint, norbit = out_ref.shape
    grid = orb_ref.shape[-1]
    out_ref[...] = jnp.zeros_like(out_ref)

    def scan(point, count):
        held = code_ref[point] >= 0

        @pl.when(held)
        def _():
            owned_ref[count] = point

        return count + held.astype(jnp.int32)

    count = lax.fori_loop(0, npoint, scan, jnp.int32(0))

    def fetch(turn):
        row = code_ref[owned_ref[turn]] // grid
        slot = lax.rem(turn, slots)
        return pltpu.make_async_copy(orb_ref.at[:, row, 0, :], buf.at[slot], sem.at[slot])

    def prime(turn, carry):
        fetch(turn).start()
        return carry

    lax.fori_loop(0, jnp.minimum(count, slots - 1), prime, 0)

    def take(turn, carry):
        @pl.when(turn + slots - 1 < count)
        def _():
            fetch(turn + slots - 1).start()

        fetch(turn).wait()
        point = owned_ref[turn]
        lane = lax.rem(code_ref[point], grid)
        hot = (lax.broadcasted_iota(jnp.int32, (8, grid), 1) == lane).astype(f32)
        column = lax.dot_general(
            hot,
            buf[lax.rem(turn, slots)],
            (((1,), (1,)), ((), ())),
            precision=highest,
            preferred_element_type=f32,
        )
        out_ref[pl.ds(point, 1), :] = column[:1]
        return carry

    lax.fori_loop(0, count, take, 0)


def pick(code, orbitals):
    norbit, grid = orbitals.shape[0], orbitals.shape[-1]
    npoint = code.shape[0]
    slots = 16
    return pl.pallas_call(
        functools.partial(pick_kernel, slots),
        out_shape=jax.ShapeDtypeStruct((npoint, norbit), f32),
        in_specs=[
            pl.BlockSpec(memory_space=pltpu.SMEM),
            pl.BlockSpec(memory_space=pl.ANY),
        ],
        out_specs=pl.BlockSpec(memory_space=pltpu.VMEM),
        scratch_shapes=[
            pltpu.SMEM((npoint,), jnp.int32),
            pltpu.VMEM((slots, norbit, grid), f32),
            pltpu.SemaphoreType.DMA((slots,)),
        ],
        compiler_params=pltpu.CompilerParams(vmem_limit_bytes=16 * MIB),
        name="pick_points",
    )(code, orbitals.reshape(norbit, -1, 1, grid))


def solve_kernel(vectors, rows_ref, rows_out, coeff_out, gram_ref, inv_ref):
    npoint = rows_ref.shape[0]
    rows = rows_ref[...]
    high, low = split(rows)
    rows_out[...] = jnp.concatenate([high, high, low], axis=1)
    corr = lax.dot_general(
        rows, rows, (((1,), (1,)), ((), ())), precision=highest, preferred_element_type=f32
    )
    gram = corr * corr
    first = lax.broadcasted_iota(jnp.int32, (npoint, npoint), 0)
    second = lax.broadcasted_iota(jnp.int32, (npoint, npoint), 1)
    eye = (first == second).astype(f32)
    mean = jnp.sum(gram * eye) / npoint
    gram = gram + 0.01 * mean * eye
    scale = 1.0 / jnp.max(jnp.sum(gram, axis=1))
    gram = gram * scale
    gram_ref[...] = gram
    inv_ref[...] = 2.0 * eye - gram

    def residual(inverse):
        ghigh, glow = split(gram_ref[...])
        ihigh, ilow = split(inverse)
        product = mul(ghigh, ihigh) + (mul(ghigh, ilow) + mul(glow, ihigh))
        return eye - product

    def go_on(state):
        turn, size = state
        return (turn < 40) & (size > 1e-5)

    def turn_of(state):
        turn, _ = state
        inverse = inv_ref[...]
        rest = residual(inverse)
        ihigh, ilow = split(inverse)
        rhigh, rlow = split(rest)
        inv_ref[...] = inverse + (mul(ihigh, rhigh) + (mul(ihigh, rlow) + mul(ilow, rhigh)))
        return turn + 1, jnp.sum(rest * rest)

    lax.while_loop(go_on, turn_of, (jnp.int32(0), f32(1.0)))

    target = eye[:vectors]
    inverse = inv_ref[...]

    def exact(left, right):
        return jnp.dot(left, right, precision=highest, preferred_element_type=f32)

    coeff = inverse[:vectors]
    for _ in range(2):
        rest = target - exact(coeff, gram_ref[...])
        coeff = coeff + exact(rest, inverse)
    coeff_out[...] = jnp.concatenate(split(coeff * scale), axis=0)


def solve(rows, vectors):
    npoint, norbit = rows.shape
    return pl.pallas_call(
        functools.partial(solve_kernel, vectors),
        out_shape=[
            jax.ShapeDtypeStruct((npoint, 3 * norbit), bf16),
            jax.ShapeDtypeStruct((2 * vectors, npoint), bf16),
        ],
        in_specs=[pl.BlockSpec(memory_space=pltpu.VMEM)],
        out_specs=[pl.BlockSpec(memory_space=pltpu.VMEM)] * 2,
        scratch_shapes=[
            pltpu.VMEM((npoint, npoint), f32),
            pltpu.VMEM((npoint, npoint), f32),
        ],
        compiler_params=pltpu.CompilerParams(vmem_limit_bytes=40 * MIB),
        name="solve_coeffs",
    )(rows)


def place(wide_count):
    me = lax.axis_index("slab") * wide_count + lax.axis_index("wide")
    return me


def greet(devices, wide_count, me):
    barrier = pltpu.get_barrier_semaphore()

    def signal(offset, carry):
        other = lax.rem(me + offset, devices)
        pl.semaphore_signal(
            barrier,
            inc=1,
            device_id=(other // wide_count, lax.rem(other, wide_count)),
            device_id_type=MESH,
        )
        return carry

    lax.fori_loop(1, devices, signal, 0)
    pl.semaphore_wait(barrier, devices - 1)


def basis(length):
    half = length // 2
    index = np.arange(length)
    freq = np.where(index <= half, index, index - half)
    angle = (index[:, None] * freq[None, :] % length) * (2.0 * math.pi / length)
    edge = (index == 0) | (index == half)
    norm = np.where(edge, math.sqrt(1.0 / length), math.sqrt(2.0 / length))
    table = np.where(index[None, :] <= half, np.cos(angle), np.sin(angle)) * norm[None, :]
    wave = freq.astype(np.float32) * np.float32(2.0 * math.pi / length)
    return table.astype(np.float32), wave * wave


def split_table(table):
    high = table.astype(ml_dtypes.bfloat16)
    low = (table - high.astype(np.float32)).astype(ml_dtypes.bfloat16)
    return high, low


def right_table(table):
    high, low = split_table(table)
    return jnp.asarray(np.block([[high, low], [high, np.zeros_like(high)]]))


def left_table(table):
    high, low = split_table(table)
    return jnp.asarray(np.block([[high, high], [low, np.zeros_like(low)]]))


def times_right(values, table):
    grid = values.shape[1]
    high, low = split(values)
    both = mul(jnp.concatenate([high, low], axis=1), table)
    return both[:, :grid] + both[:, grid:]


def times_left(table, values):
    grid = values.shape[0]
    high, low = split(values)
    both = mul(table, jnp.concatenate([high, low], axis=0))
    return both[:grid] + both[grid:]


def fused_kernel(
    slab_count,
    wide_count,
    steps,
    orb_ref,
    rows_ref,
    coeff_ref,
    rforth_ref,
    rback_ref,
    lforth_ref,
    lback_ref,
    col_ref,
    row_ref,
    out_ref,
    buf,
    work,
    own_sem,
    send_sem,
    recv_sem,
    back_send_sem,
    back_recv_sem,
):
    devices, depth, rows, grid = buf.shape
    norbit, tall, _ = orb_ref.shape
    planes = depth // steps
    step = pl.program_id(0)
    me = place(wide_count)
    slab, wide = lax.axis_index("slab"), lax.axis_index("wide")

    @pl.when(step == 0)
    def _():
        greet(devices, wide_count, me)

    group = math.gcd(tall, 8)

    def block(turn, carry):
        base = turn * group
        cells = jnp.concatenate([orb_ref[:, base + j, :] for j in range(group)], axis=1)
        high, low = split(cells)
        pairs = mul(rows_ref[...], jnp.concatenate([high, low, high], axis=0))
        phigh, plow = split(pairs * pairs)
        main = mul(coeff_ref[...], phigh)
        piece = main[:devices] + (main[devices:] + mul(coeff_ref[:devices], plow))
        first = step * tall + base
        for j in range(group):
            row = first + j
            buf[:, row // rows, lax.rem(row, rows), :] = piece[:, j * grid : (j + 1) * grid]
        return carry

    lax.fori_loop(0, tall // group, block, 0)

    def send(offset, carry):
        other = lax.rem(me + offset, devices)
        pltpu.make_async_remote_copy(
            src_ref=buf.at[other, pl.ds(step * planes, planes)],
            dst_ref=work.at[pl.ds(slab * depth + step * planes, planes), wide],
            send_sem=send_sem,
            recv_sem=recv_sem.at[step],
            device_id=(other // wide_count, lax.rem(other, wide_count)),
            device_id_type=MESH,
        ).start()
        return carry

    lax.fori_loop(1, devices, send, 0)

    @pl.when(step == steps - 1)
    def _():
        transform(
            slab_count,
            wide_count,
            steps,
            rforth_ref,
            rback_ref,
            lforth_ref,
            lback_ref,
            col_ref,
            row_ref,
            out_ref,
            buf,
            work,
            own_sem,
            send_sem,
            recv_sem,
            back_send_sem,
            back_recv_sem,
        )


def transform(
    slab_count,
    wide_count,
    steps,
    rforth_ref,
    rback_ref,
    lforth_ref,
    lback_ref,
    col_ref,
    row_ref,
    out_ref,
    buf,
    work,
    own_sem,
    send_sem,
    recv_sem,
    back_send_sem,
    back_recv_sem,
):
    devices, depth, rows, grid = buf.shape
    planes = depth // steps
    me = place(wide_count)
    slab, wide = lax.axis_index("slab"), lax.axis_index("wide")

    def side_by_side(values):
        return jnp.concatenate(
            [values[j * grid : (j + 1) * grid] for j in range(values.shape[0] // grid)], axis=1
        )

    def stacked(values):
        return jnp.concatenate(
            [values[:, j * grid : (j + 1) * grid] for j in range(values.shape[1] // grid)], axis=0
        )

    def forth(turn, carry):
        arrived = buf.at[pl.ds(0, devices - 1), pl.ds(0, planes)]
        pltpu.make_async_copy(arrived, arrived, recv_sem.at[turn]).wait()
        local = pl.ds(turn * planes, planes)
        work[pl.ds(slab * depth + turn * planes, planes), wide] = buf[me, local]
        places = [pl.ds(at * depth + turn * planes, planes) for at in range(slab_count)]
        values = jnp.concatenate(
            [work[at].reshape(planes * grid, grid) for at in places], axis=0
        )
        along_x = times_right(values, rforth_ref[...])
        along_y = stacked(times_left(lforth_ref[...], side_by_side(along_x)))
        for at in range(slab_count):
            piece = along_y[at * planes * grid : (at + 1) * planes * grid]
            work[places[at]] = piece.reshape(planes, wide_count, rows, grid)
        return carry

    lax.fori_loop(0, steps, forth, 0)

    batch = math.gcd(rows, 8)

    def middle(turn, carry):
        base = turn * batch
        of_wide = base // rows
        of_row = lax.rem(base, rows)
        values = jnp.concatenate(
            [work[:, of_wide, of_row + j, :] for j in range(batch)], axis=1
        )
        spectrum = times_left(lforth_ref[...], values)
        pieces = []
        for j in range(batch):
            yfreq = col_ref[pl.ds(base + j, 1), :]
            total = (col_ref[...] + yfreq) + row_ref[...]
            safe = jnp.where(total > 0, total, 1.0)
            kernel = jnp.where(total > 0, (4.0 * math.pi) / safe, 0.0)
            pieces.append(spectrum[:, j * grid : (j + 1) * grid] * kernel)
        back = times_left(lback_ref[...], jnp.concatenate(pieces, axis=1))
        for j in range(batch):
            work[:, of_wide, of_row + j, :] = back[:, j * grid : (j + 1) * grid]
        return carry

    lax.fori_loop(0, grid // batch, middle, 0)

    others = buf.at[pl.ds(0, devices - 1)]
    pltpu.make_async_copy(others, others, send_sem).wait()
    count = math.gcd(depth, 4)

    def finish(turn, carry):
        to_slab = lax.rem(turn + slab + 1, slab_count)
        inner = (turn // slab_count) * count
        values = work[pl.ds(to_slab * depth + inner, count)].reshape(count * grid, grid)
        along_y = stacked(times_left(lback_ref[...], side_by_side(values)))
        field = times_right(along_y, rback_ref[...]).reshape(count, wide_count, rows, grid)
        for to_wide in range(wide_count):
            buf[to_slab * wide_count + to_wide, pl.ds(inner, count)] = field[:, to_wide]

        def send(offset, inner_carry):
            to_wide = lax.rem(wide + offset, wide_count)

            @pl.when((to_slab != slab) | (to_wide != wide))
            def _():
                pltpu.make_async_remote_copy(
                    src_ref=buf.at[to_slab * wide_count + to_wide, pl.ds(inner, count)],
                    dst_ref=out_ref.at[me, pl.ds(inner, count)],
                    send_sem=back_send_sem,
                    recv_sem=back_recv_sem,
                    device_id=(to_slab, to_wide),
                    device_id_type=MESH,
                ).start()

            return inner_carry

        lax.fori_loop(1, wide_count + 1, send, 0)
        return carry

    lax.fori_loop(0, grid // count, finish, 0)

    mine = pltpu.make_async_copy(buf.at[me], out_ref.at[me], own_sem)
    mine.start()
    mine.wait()
    pltpu.make_async_copy(others, others, back_send_sem).wait()
    pltpu.make_async_copy(others, others, back_recv_sem).wait()


def potentials(orbitals, rows_cat, coeff_cat, slab_count, wide_count):
    norbit, depth, rows, grid = orbitals.shape
    devices = slab_count * wide_count
    tall = max(rows, math.gcd(depth * rows, 32))
    steps = depth * rows // tall
    table, squares = basis(grid)
    tables = [right_table(table), right_table(table.T), left_table(table.T), left_table(table)]
    column = jnp.asarray(np.broadcast_to(squares[:, None], (grid, grid)))
    line = jnp.asarray(squares[None, :])
    vmem = pl.BlockSpec(memory_space=pltpu.VMEM)
    return pl.pallas_call(
        functools.partial(fused_kernel, slab_count, wide_count, steps),
        grid=(steps,),
        out_shape=jax.ShapeDtypeStruct((devices, depth, rows, grid), f32),
        in_specs=[pl.BlockSpec((norbit, tall, grid), lambda step: (0, step, 0))] + [vmem] * 8,
        out_specs=pl.BlockSpec(memory_space=pl.ANY),
        scratch_shapes=[
            pltpu.VMEM((devices, depth, rows, grid), f32),
            pltpu.VMEM((grid, wide_count, rows, grid), f32),
            pltpu.SemaphoreType.DMA,
            pltpu.SemaphoreType.DMA,
            pltpu.SemaphoreType.DMA((steps,)),
            pltpu.SemaphoreType.DMA,
            pltpu.SemaphoreType.DMA,
        ],
        compiler_params=pltpu.CompilerParams(
            collective_id=0, has_side_effects=True, vmem_limit_bytes=56 * MIB
        ),
        name="fit_and_transform",
    )(orbitals.reshape(norbit, depth * rows, grid), rows_cat, coeff_cat, *tables, column, line)


def per_device(orbitals, points):
    norbit, depth, rows, grid = orbitals.shape
    slab_count = lax.axis_size("slab")
    wide_count = lax.axis_size("wide")
    slab_index = lax.axis_index("slab")
    wide_index = lax.axis_index("wide")
    zcoord = points // (grid * grid)
    ycoord = points // grid % grid
    xcoord = points % grid
    owned = (zcoord // depth == slab_index) & (ycoord // rows == wide_index)
    offset = ((zcoord - slab_index * depth) * rows + (ycoord - wide_index * rows)) * grid + xcoord
    code = jnp.where(owned, offset, -1).astype(jnp.int32)
    sampled_rows = lax.psum(pick(code, orbitals), ("slab", "wide"))
    devices = slab_count * wide_count
    rows_cat, coeff_cat = solve(sampled_rows, devices)
    return potentials(orbitals, rows_cat, coeff_cat, slab_count, wide_count)


def solution(mesh):
    placed = (P(None, "slab", "wide", None), P())
    return jax.shard_map(
        per_device,
        mesh=mesh,
        in_specs=placed,
        out_specs=P(None, "slab", "wide", None),
        check_vma=False,
    )
```

time: 1320 us -> 591 us (0.45)
  matrix products: 533 us -> 0 us
  Pallas kernels: 0 us -> 444 us
  waiting for transfers between devices: 316 us -> 124 us
  blocking collectives: 187 us -> 0 us
  other arithmetic: 135 us -> 0.71 us
  local copies, waits for them, and re-layouts: 122 us -> 10.9 us
    dot_general x53 -> x0, matrix products: 528 us -> none  [the longest x20 249 us: contract(): jnp.einsum(letters + ',' + letters[axis_pos] + 'k->' + target, values, ta...]
    pallas_call x0 -> x3, Pallas kernels: none -> 444 us  [the longest x1 392 us: potentials(): pl.pallas_call(functools.partial(fused_kernel, slab_count, wide_count, st...]
    all_to_all x1 -> x0, blocking collectives: 187 us -> none  [per_device(): lax.all_to_all(back, ('slab', 'wide'), split_axis=1, concat_axis=0, tiled...]
    all_to_all x1 -> x0, waiting for transfers between devices: 183 us -> none  [per_device(): lax.all_to_all(shaped, ('slab', 'wide'), split_axis=0, concat_axis=1, til...]
    another operation x17 -> x0, other arithmetic: 118 us -> none  [the longest x14 78.8 us: per_device(): factor = jnp.linalg.cholesky(gram)]
    unnamed x13 -> x9, local copies, waits for them, and re-layouts: 78.3 us -> 10.2 us
    gather x2 -> x0, local copies, waits for them, and re-layouts: 22 us -> none  [the longest x1 17.3 us: per_device(): picked = jnp.take(flat, offset, axis=1) * owned.astype(jnp.float32)[None, :]]
  transfers between devices with their start and end apart: 2 -> 1, of which waited for: 2 -> 1; matrix products, arithmetic and copies ran while one was open for 1% -> 0% of each run, Pallas kernels for 0% -> 0%
where the time goes in v1:
time: 591 us; the launch traced here: 593 us
  Pallas kernels  444 us (75%)
  waiting for transfers between devices  124 us (21%)
  between operations  13.4 us (2%)
  local copies, waits for them, and re-layouts  10.9 us (2%)
    pallas_call x1, Pallas kernels, potentials(): pl.pallas_call(functools.partial(fused_kernel, slab_count, wide_count, st...  392 us
    psum x1, waiting for transfers between devices, per_device(): sampled_rows = lax.psum(pick(code, orbitals), ('slab', 'wide'))  124 us
    pallas_call x1, Pallas kernels, pick(): pl.pallas_call(functools.partial(pick_kernel, slots), out_shape=jax.Shape...  28 us
    pallas_call x1, Pallas kernels, solve(): pl.pallas_call(functools.partial(solve_kernel, vectors), out_shape=[jax.S...  23.3 us
  transfers between devices with their start and end apart: 1, of which 1 were waited for; matrix products, arithmetic and copies ran while one was open for 0% of the time, Pallas kernels for 0%

profile of v1, /device:TPU:0, one launch (start us, length us, event | category | flops | bytes accessed | tf_op | source)
XLA Modules:
  0.0 592.7 jit_solution(4971868930554407793)
XLA Ops:
  6.5 0.0 all-reduce.2.cloned.1.call-start
  6.5 0.7 fusion.7.code_ref
  7.2 0.0 copy-start.3
  7.3 28.0 %pick_points.1 = f32[512,256]{1,0:T(8,128)} custom-call(s32[512]{0:T(512)S(1)} %fusion.7.code_ref, f32[256,512,1,128]{3,2,1,0:T(1,128)} %bitcast.1.orb_ref), custom_call_target="tpu_custom_call" | custom-call | tf_op jit(solution)/shard_map/pick_points/pallas_call | solution.py:83
  35.3 0.0 all-reduce.2.cloned.1.call-update
  35.3 123.9 %all-reduce.2.cloned.1.call-done.rows_ref = f32[512,256]{1,0:T(8,128)} async-done(((f32[512,256]{1,0:T(8,128)}), f32[512,256]{1,0:T(8,128)}) %all-reduce.2.cloned.1.call-update) | async-done | bytes 524304 | tf_op jit(solution)/shard_map/psum | solution.py:486
  159.2 0.0 copy-start.1
  159.2 1.0 copy-done.1
  160.2 23.3 %solve_coeffs.1 = (bf16[512,768]{1,0:T(8,128)(2,1)S(1)}, bf16[64,512]{1,0:T(8,128)(2,1)S(1)}) custom-call(f32[512,256]{1,0:T(8,128)S(1)} %copy-done.1), custom_call_target="tpu_custom_call" | custom-call | tf_op jit(solution)/shard_map/solve_coeffs/pallas_call | solution.py:156
  183.5 0.0 copy-start
  183.6 0.9 copy-done
  184.4 0.0 copy-start.2
  184.4 0.6 copy-done.2
  185.0 0.0 copy-done.3
  185.1 0.7 jit_solution_.3.col_ref
  185.8 392.5 %fit_and_transform.1 = f32[32,32,16,128]{3,2,1,0:T(8,128)} custom-call(f32[256,512,128]{2,1,0:T(8,128)} %bitcast.orb_ref, bf16[512,768]{1,0:T(8,128)(2,1)} %copy-done, bf16[64,512]{1,0:T(8,128)(2,1)} %copy-done.2, bf16[256,256]{1,0:T(8,128)(2,1)} %constant.91.clone.rforth_ref, bf16[256,256]{1,0:T(8,128)(2,1)} %constant.92.clone.rback_ref, ...), custom_call_target="tpu_custom_call" | custom-call | tf_op jit(solution)/shard_map/fit_and_transform/pallas_call | solution.py:452
  578.2 7.7 %copy.11 = f32[32,32,16,128]{3,2,1,0:T(8,128)} copy(f32[32,32,16,128]{3,2,1,0:T(8,128)} %fit_and_transform.1) | data formatting | bytes 16777216
Async XLA Ops:
  6.5 152.7 %all-reduce.2.cloned.1.call-start = ((), (), s32[]{:S(2)}) async-start(), calls=%async_computation | async-start | bytes 1048576 | tf_op jit(solution)/shard_map/psum | solution.py:486
  7.2 177.8 %copy-start.3 = (f32[128]{0:T(128)S(1)}, f32[128]{0:T(128)}, u32[]{:S(2)}) copy-start(f32[128]{0:T(128)} %constant.95.clone) | copy-start | bytes 1540
  159.2 1.0 copy-start.1
  183.5 0.9 copy-start
  184.4 0.6 copy-start.2
Sparse Core Ops, SparseCore 0:
  35.5 123.6 all-reduce.1

commit v2 on v1

--- a/solution.py
+++ b/solution.py
@@ -28,20 +28,14 @@
 
 
 def pick_kernel(slots, code_ref, orb_ref, out_ref, owned_ref, buf, sem):
-    npoint, norbit = out_ref.shape
-    grid = orb_ref.shape[-1]
+    blocks, norbit, grid = out_ref.shape
     out_ref[...] = jnp.zeros_like(out_ref)
 
     def scan(point, count):
-        held = code_ref[point] >= 0
-
-        @pl.when(held)
-        def _():
-            owned_ref[count] = point
-
-        return count + held.astype(jnp.int32)
-
-    count = lax.fori_loop(0, npoint, scan, jnp.int32(0))
+        owned_ref[count] = point
+        return count + (code_ref[point] >= 0).astype(jnp.int32)
+
+    count = lax.fori_loop(0, blocks * grid, scan, jnp.int32(0), unroll=8)
 
     def fetch(turn):
         row = code_ref[owned_ref[turn]] // grid
@@ -53,6 +47,7 @@
         return carry
 
     lax.fori_loop(0, jnp.minimum(count, slots - 1), prime, 0)
+    lanes = lax.broadcasted_iota(jnp.int32, (norbit, grid), 1)
 
     def take(turn, carry):
         @pl.when(turn + slots - 1 < count)
@@ -62,15 +57,10 @@
         fetch(turn).wait()
         point = owned_ref[turn]
         lane = lax.rem(code_ref[point], grid)
-        hot = (lax.broadcasted_iota(jnp.int32, (8, grid), 1) == lane).astype(f32)
-        column = lax.dot_general(
-            hot,
-            buf[lax.rem(turn, slots)],
-            (((1,), (1,)), ((), ())),
-            precision=highest,
-            preferred_element_type=f32,
-        )
-        out_ref[pl.ds(point, 1), :] = column[:1]
+        target = lax.rem(point, grid)
+        moved = pltpu.roll(buf[lax.rem(turn, slots)], lax.rem(target - lane + grid, grid), 1)
+        of_block = point // grid
+        out_ref[of_block] = jnp.where(lanes == target, moved, out_ref[of_block])
         return carry
 
     lax.fori_loop(0, count, take, 0)
@@ -82,7 +72,7 @@
     slots = 16
     return pl.pallas_call(
         functools.partial(pick_kernel, slots),
-        out_shape=jax.ShapeDtypeStruct((npoint, norbit), f32),
+        out_shape=jax.ShapeDtypeStruct((npoint // grid, norbit, grid), f32),
         in_specs=[
             pl.BlockSpec(memory_space=pltpu.SMEM),
             pl.BlockSpec(memory_space=pl.ANY),
@@ -98,9 +88,68 @@
     )(code, orbitals.reshape(norbit, -1, 1, grid))
 
 
+def sum_kernel(wide_count, part_ref, out_ref, parts, whole, sems):
+    devices = part_ref.shape[0]
+    me = place(wide_count)
+    greet(devices, wide_count, me)
+
+    def copy_to(offset, source, target, first):
+        other = lax.rem(me + offset, devices)
+        pltpu.make_async_remote_copy(
+            src_ref=source(other),
+            dst_ref=target.at[me],
+            send_sem=sems.at[first],
+            recv_sem=sems.at[first + 1],
+            device_id=(other // wide_count, lax.rem(other, wide_count)),
+            device_id_type=MESH,
+        ).start()
+
+    def scatter(offset, carry):
+        copy_to(offset, lambda other: part_ref.at[other], parts, 0)
+        return carry
+
+    def gather(offset, carry):
+        copy_to(offset, lambda other: whole.at[me], whole, 2)
+        return carry
+
+    lax.fori_loop(1, devices, scatter, 0)
+    parts[me] = part_ref[me]
+    others = parts.at[pl.ds(0, devices - 1)]
+    pltpu.make_async_copy(others, others, sems.at[1]).wait()
+    whole[me] = jnp.sum(parts[...], axis=0)
+    lax.fori_loop(1, devices, gather, 0)
+    pltpu.make_async_copy(others, others, sems.at[3]).wait()
+    out_ref[...] = whole[...]
+    pltpu.make_async_copy(others, others, sems.at[0]).wait()
+    pltpu.make_async_copy(others, others, sems.at[2]).wait()
+
+
+def sum_over(picked, slab_count, wide_count):
+    devices = slab_count * wide_count
+    grid = picked.shape[-1]
+    shape = (devices, picked.size // (devices * grid), grid)
+    vmem = pl.BlockSpec(memory_space=pltpu.VMEM)
+    total = pl.pallas_call(
+        functools.partial(sum_kernel, wide_count),
+        out_shape=jax.ShapeDtypeStruct(shape, f32),
+        in_specs=[vmem],
+        out_specs=vmem,
+        scratch_shapes=[
+            pltpu.VMEM(shape, f32),
+            pltpu.VMEM(shape, f32),
+            pltpu.SemaphoreType.DMA((4,)),
+        ],
+        compiler_params=pltpu.CompilerParams(
+            collective_id=1, has_side_effects=True, vmem_limit_bytes=16 * MIB
+        ),
+        name="sum_picked",
+    )(picked.reshape(shape))
+    return total.reshape(picked.shape)
+
+
 def solve_kernel(vectors, rows_ref, rows_out, coeff_out, gram_ref, inv_ref):
-    npoint = rows_ref.shape[0]
-    rows = rows_ref[...]
+    npoint = gram_ref.shape[0]
+    rows = jnp.concatenate([rows_ref[at] for at in range(rows_ref.shape[0])], axis=1).T
     high, low = split(rows)
     rows_out[...] = jnp.concatenate([high, high, low], axis=1)
     corr = lax.dot_general(
@@ -152,7 +201,8 @@
 
 
 def solve(rows, vectors):
-    npoint, norbit = rows.shape
+    blocks, norbit, grid = rows.shape
+    npoint = blocks * grid
     return pl.pallas_call(
         functools.partial(solve_kernel, vectors),
         out_shape=[
@@ -483,9 +533,8 @@
     owned = (zcoord // depth == slab_index) & (ycoord // rows == wide_index)
     offset = ((zcoord - slab_index * depth) * rows + (ycoord - wide_index * rows)) * grid + xcoord
     code = jnp.where(owned, offset, -1).astype(jnp.int32)
-    sampled_rows = lax.psum(pick(code, orbitals), ("slab", "wide"))
-    devices = slab_count * wide_count
-    rows_cat, coeff_cat = solve(sampled_rows, devices)
+    sampled = sum_over(pick(code, orbitals), slab_count, wide_count)
+    rows_cat, coeff_cat = solve(sampled, slab_count * wide_count)
     return potentials(orbitals, rows_cat, coeff_cat, slab_count, wide_count)
 
 

time: 591 us -> 469 us (0.79)
  waiting for transfers between devices: 124 us -> 0 us
  between operations: 13.4 us -> 0.05 us
  Pallas kernels: 444 us -> 457 us
    psum x1 -> x0, waiting for transfers between devices: 124 us -> none  [per_device(): sampled_rows = lax.psum(pick(code, orbitals), ('slab', 'wide'))]
    pallas_call x0 -> x1, Pallas kernels: none -> 27.7 us  [sum_over(): pl.pallas_call(functools.partial(sum_kernel, wide_count), out_shape=jax.S...]
    pallas_call x1, Pallas kernels: 28 us -> 14.6 us  [pick(): pl.pallas_call(functools.partial(pick_kernel, slots), out_shape=jax.Shape...]
  transfers between devices with their start and end apart: 1 -> 0, of which waited for: 1 -> 0; matrix products, arithmetic and copies ran while one was open for 0% -> 0% of each run, Pallas kernels for 0% -> 0%
where the time goes in v2:
time: 469 us; the launch traced here: 468 us
  Pallas kernels  457 us (97%)
  local copies, waits for them, and re-layouts  9.85 us (2%)
    pallas_call x1, Pallas kernels, potentials(): pl.pallas_call(functools.partial(fused_kernel, slab_count, wide_count, st...  394 us
    pallas_call x1, Pallas kernels, sum_over(): pl.pallas_call(functools.partial(sum_kernel, wide_count), out_shape=jax.S...  27.7 us
    pallas_call x1, Pallas kernels, solve(): pl.pallas_call(functools.partial(solve_kernel, vectors), out_shape=[jax.S...  21.5 us
    pallas_call x1, Pallas kernels, pick(): pl.pallas_call(functools.partial(pick_kernel, slots), out_shape=jax.Shape...  14.6 us

profile of v2, /device:TPU:0, one launch (start us, length us, event | category | flops | bytes accessed | tf_op | source)
XLA Modules:
  0.0 468.1 jit_solution(309123463943185494)
XLA Ops:
  0.0 0.7 fusion.7.code_ref
  0.7 0.0 copy-start.2
  0.7 14.6 %pick_points.1 = f32[4,256,128]{2,1,0:T(8,128)S(1)} custom-call(s32[512]{0:T(512)S(1)} %fusion.7.code_ref, f32[256,512,1,128]{3,2,1,0:T(1,128)} %bitcast.1.orb_ref), custom_call_target="tpu_custom_call" | custom-call | tf_op jit(solution)/shard_map/pick_points/pallas_call | solution.py:73
  15.3 27.7 %sum_picked.1 = f32[32,32,128]{2,1,0:T(8,128)S(1)} custom-call(f32[32,32,128]{2,1,0:T(8,128)S(1)} %bitcast.4), custom_call_target="tpu_custom_call" | custom-call | tf_op jit(solution)/shard_map/sum_picked/pallas_call | solution.py:132
  43.0 21.5 %solve_coeffs.1 = (bf16[512,768]{1,0:T(8,128)(2,1)S(1)}, bf16[64,512]{1,0:T(8,128)(2,1)S(1)}) custom-call(f32[4,256,128]{2,1,0:T(8,128)S(1)} %bitcast.5), custom_call_target="tpu_custom_call" | custom-call | tf_op jit(solution)/shard_map/solve_coeffs/pallas_call | solution.py:206
  64.6 0.0 copy-start
  64.6 0.9 copy-done
  65.5 0.0 copy-start.1
  65.5 0.6 copy-done.1
  66.1 0.0 copy-done.2
  66.1 0.7 jit_solution_.3.col_ref
  66.8 393.7 %fit_and_transform.1 = f32[32,32,16,128]{3,2,1,0:T(8,128)} custom-call(f32[256,512,128]{2,1,0:T(8,128)} %bitcast.orb_ref, bf16[512,768]{1,0:T(8,128)(2,1)} %copy-done, bf16[64,512]{1,0:T(8,128)(2,1)} %copy-done.1, bf16[256,256]{1,0:T(8,128)(2,1)} %constant.91.clone.rforth_ref, bf16[256,256]{1,0:T(8,128)(2,1)} %constant.92.clone.rback_ref, ...), custom_call_target="tpu_custom_call" | custom-call | tf_op jit(solution)/shard_map/fit_and_transform/pallas_call | solution.py:502
  460.5 7.7 %copy.10 = f32[32,32,16,128]{3,2,1,0:T(8,128)} copy(f32[32,32,16,128]{3,2,1,0:T(8,128)} %fit_and_transform.1) | data formatting | bytes 16777216
Async XLA Ops:
  0.7 65.4 %copy-start.2 = (f32[128]{0:T(128)S(1)}, f32[128]{0:T(128)}, u32[]{:S(2)}) copy-start(f32[128]{0:T(128)} %constant.95.clone) | copy-start | bytes 1540
  64.6 0.9 copy-start
  65.5 0.6 copy-start.1

commit v3 on v2

--- a/solution.py
+++ b/solution.py
@@ -335,22 +335,40 @@
 
     lax.fori_loop(0, tall // group, block, 0)
 
-    def send(offset, carry):
-        other = lax.rem(me + offset, devices)
-        pltpu.make_async_remote_copy(
-            src_ref=buf.at[other, pl.ds(step * planes, planes)],
-            dst_ref=work.at[pl.ds(slab * depth + step * planes, planes), wide],
-            send_sem=send_sem,
-            recv_sem=recv_sem.at[step],
-            device_id=(other // wide_count, lax.rem(other, wide_count)),
-            device_id_type=MESH,
-        ).start()
-        return carry
-
-    lax.fori_loop(1, devices, send, 0)
+    lag = steps // 4
+
+    def send_step(which, parity):
+        def send(offset, carry):
+            other = lax.rem(me + offset, devices)
+
+            @pl.when(lax.rem(other // wide_count, 2) == parity)
+            def _():
+                pltpu.make_async_remote_copy(
+                    src_ref=buf.at[other, pl.ds(which * planes, planes)],
+                    dst_ref=work.at[pl.ds(slab * depth + which * planes, planes), wide],
+                    send_sem=send_sem,
+                    recv_sem=recv_sem.at[which],
+                    device_id=(other // wide_count, lax.rem(other, wide_count)),
+                    device_id_type=MESH,
+                ).start()
+
+            return carry
+
+        lax.fori_loop(1, devices, send, 0)
+
+    send_step(step, 0)
+
+    @pl.when(step >= lag)
+    def _():
+        send_step(step - lag, 1)
 
     @pl.when(step == steps - 1)
     def _():
+        def send_late(which, carry):
+            send_step(which, 1)
+            return carry
+
+        lax.fori_loop(steps - lag, steps, send_late, 0)
         transform(
             slab_count,
             wide_count,

time: 469 us -> 467 us (level)
  no operation moved by 1% of the time
where the time goes in v3:
time: 467 us; the launch traced here: 466 us
  Pallas kernels  455 us (97%)
  local copies, waits for them, and re-layouts  9.85 us (2%)
    pallas_call x1, Pallas kernels, potentials(): pl.pallas_call(functools.partial(fused_kernel, slab_count, wide_count, st...  391 us
    pallas_call x1, Pallas kernels, sum_over(): pl.pallas_call(functools.partial(sum_kernel, wide_count), out_shape=jax.S...  27.7 us
    pallas_call x1, Pallas kernels, solve(): pl.pallas_call(functools.partial(solve_kernel, vectors), out_shape=[jax.S...  19.6 us
    pallas_call x1, Pallas kernels, pick(): pl.pallas_call(functools.partial(pick_kernel, slots), out_shape=jax.Shape...  16.3 us

profile of v3, /device:TPU:0, one launch (start us, length us, event | category | flops | bytes accessed | tf_op | source)
XLA Modules:
  0.0 465.7 jit_solution(4503640005852248012)
XLA Ops:
  0.0 0.7 fusion.7.code_ref
  0.7 0.0 copy-start.2
  0.7 16.3 %pick_points.1 = f32[4,256,128]{2,1,0:T(8,128)S(1)} custom-call(s32[512]{0:T(512)S(1)} %fusion.7.code_ref, f32[256,512,1,128]{3,2,1,0:T(1,128)} %bitcast.1.orb_ref), custom_call_target="tpu_custom_call" | custom-call | tf_op jit(solution)/shard_map/pick_points/pallas_call | solution.py:73
  17.1 27.7 %sum_picked.1 = f32[32,32,128]{2,1,0:T(8,128)S(1)} custom-call(f32[32,32,128]{2,1,0:T(8,128)S(1)} %bitcast.4), custom_call_target="tpu_custom_call" | custom-call | tf_op jit(solution)/shard_map/sum_picked/pallas_call | solution.py:132
  44.8 19.6 %solve_coeffs.1 = (bf16[512,768]{1,0:T(8,128)(2,1)S(1)}, bf16[64,512]{1,0:T(8,128)(2,1)S(1)}) custom-call(f32[4,256,128]{2,1,0:T(8,128)S(1)} %bitcast.5), custom_call_target="tpu_custom_call" | custom-call | tf_op jit(solution)/shard_map/solve_coeffs/pallas_call | solution.py:206
  64.4 0.0 copy-start
  64.4 0.9 copy-done
  65.3 0.0 copy-start.1
  65.3 0.6 copy-done.1
  65.9 0.0 copy-done.2
  65.9 0.7 jit_solution_.3.col_ref
  66.6 391.4 %fit_and_transform.1 = f32[32,32,16,128]{3,2,1,0:T(8,128)} custom-call(f32[256,512,128]{2,1,0:T(8,128)} %bitcast.orb_ref, bf16[512,768]{1,0:T(8,128)(2,1)} %copy-done, bf16[64,512]{1,0:T(8,128)(2,1)} %copy-done.1, bf16[256,256]{1,0:T(8,128)(2,1)} %constant.91.clone.rforth_ref, bf16[256,256]{1,0:T(8,128)(2,1)} %constant.92.clone.rback_ref, ...), custom_call_target="tpu_custom_call" | custom-call | tf_op jit(solution)/shard_map/fit_and_transform/pallas_call | solution.py:520
  458.0 7.7 %copy.10 = f32[32,32,16,128]{3,2,1,0:T(8,128)} copy(f32[32,32,16,128]{3,2,1,0:T(8,128)} %fit_and_transform.1) | data formatting | bytes 16777216
Async XLA Ops:
  0.7 65.2 %copy-start.2 = (f32[128]{0:T(128)S(1)}, f32[128]{0:T(128)}, u32[]{:S(2)}) copy-start(f32[128]{0:T(128)} %constant.95.clone) | copy-start | bytes 1540
  64.4 0.9 copy-start
  65.3 0.6 copy-start.1
